TPU v7x, 32 devices: a whole 2x2x4 slice. The times are simulated.
32 devices in a mesh: gx: 16 (over z, y, core), gy: 2 (over x).
Axes of the slice: x: 2, y: 2, z: 4, core: 2. Of those that a mesh axis runs over, the one named last changes fastest.
Arguments:
- latents: int32 [768, 64, 32], P('gy', 'gx'), may hold values from 0 to 31
- actions: int32 [768, 64], P('gy', 'gx'), may hold values from 0 to 17
- segment_ids: int32 [768, 64], replicated, may hold values from 0 to 3, never falling along the last dimension, each value on 1 to 32 neighbouring positions
- cotangent: bfloat16 [768, 64, 512], P('gy', 'gx'), may hold values from -6 to 6
- stem_weight: bfloat16 [1024, 512], replicated, may hold values from -1 to 1
- action_table: bfloat16 [18, 512], replicated, may hold values from -1 to 1
- first_gain: float32 [512], replicated, may hold values from 0.5 to 1.5
- first_bias: float32 [512], replicated, may hold values from -1 to 1
- query_weight: bfloat16 [512, 512], P(None, 'gy'), may hold values from -0.25 to 0.25
- key_weight: bfloat16 [512, 512], P(None, 'gy'), may hold values from -0.25 to 0.25
- value_weight: bfloat16 [512, 512], P(None, 'gy'), may hold values from -0.25 to 0.25
- out_weight: bfloat16 [512, 512], P('gy'), may hold values from -1 to 1
- second_gain: float32 [512], replicated, may hold values from 0.5 to 1.5
- second_bias: float32 [512], replicated, may hold values from -1 to 1
- up_weight: bfloat16 [512, 2048], P(None, 'gy'), may hold values from -0.25 to 0.25
- up_bias: float32 [2048], P('gy'), may hold values from -1 to 1
- down_weight: bfloat16 [2048, 512], P('gy'), may hold values from -0.125 to 0.125
- down_bias: float32 [512], replicated, may hold values from -1 to 1
Outputs:
- output: bfloat16 [768, 64, 512], P('gy', 'gx')
- token_grad: bfloat16 [768, 64, 512], P('gy', 'gx')
- stem_grad: float32 [1024, 512], replicated
- action_grad: float32 [18, 512], replicated
- first_gain_grad: float32 [512], replicated
- first_bias_grad: float32 [512], replicated
- query_grad: float32 [512, 512], P(None, 'gy')
- key_grad: float32 [512, 512], P(None, 'gy')
- value_grad: float32 [512, 512], P(None, 'gy')
- out_grad: float32 [512, 512], P('gy')
- second_gain_grad: float32 [512], replicated
- second_bias_grad: float32 [512], replicated
- up_grad: float32 [512, 2048], P(None, 'gy')
- up_bias_grad: float32 [2048], P('gy')
- down_grad: float32 [2048, 512], P('gy')
- down_bias_grad: float32 [512], replicated
Inputs may be any that keep to these rules, and one draw needn't show every extreme that they name: `segment_ids`: along each sequence of 64 frames the segment id never falls; each segment holds 1 to 32 frames.
All inputs are finite; a program needn't handle non-finite values.
Results may differ from a plain program's by a relative error of at most 0.012.
Values may be sent and summed in bfloat16 or wider, within the bound.
A program may use at most 192 MiB of HBM per device.

v0:
```python
import jax
import jax.numpy as jnp
from jax import lax
from jax.sharding import PartitionSpec as P

HD = 64
EPSILON = 1e-05
FLOAT = jnp.float32
BFLOAT = jnp.bfloat16


def norm_rows(values, gain, bias):
    average = jnp.mean(values, axis=-1, keepdims=True)
    centred = values - average
    spread = jnp.mean(centred * centred, axis=-1, keepdims=True)
    return centred * lax.rsqrt(spread + EPSILON) * gain + bias


def inner(left, right):
    return lax.dot_general(left, right, (((0,), (0,)), ((), ())), preferred_element_type=FLOAT)


def outer(left, right):
    return lax.dot_general(left, right, (((1,), (1,)), ((), ())), preferred_element_type=FLOAT)


def product(left, right):
    return jnp.dot(left, right, preferred_element_type=FLOAT)


def split_heads(block):
    return block.reshape(block.shape[0], block.shape[1], -1, HD)


def block_probs(query_block, key_block, label_block):
    length = query_block.shape[1]
    scores = 0.125 * jnp.einsum(
        "sqhd,skhd->shqk",
        split_heads(query_block),
        split_heads(key_block),
        preferred_element_type=FLOAT,
    )
    place = jnp.arange(length)
    allowed = (label_block[:, :, None] == label_block[:, None, :]) & (
        place[:, None] >= place[None, :]
    )[None]
    return jax.nn.softmax(jnp.where(allowed[:, None], scores, -1e30), axis=-1)


def block_forward(pieces):
    query_block, key_block, value_block, label_block = pieces
    probs_low = block_probs(query_block, key_block, label_block).astype(BFLOAT)
    mixed = jnp.einsum(
        "shqk,skhd->sqhd", probs_low, split_heads(value_block), preferred_element_type=FLOAT
    )
    return mixed.reshape(query_block.shape[0], query_block.shape[1], -1).astype(BFLOAT)


def block_backward(pieces):
    query_block, key_block, value_block, label_block, grad_block = pieces
    probs = block_probs(query_block, key_block, label_block)
    grad_heads = split_heads(grad_block)
    grad_probs = jnp.einsum(
        "sqhd,skhd->shqk", grad_heads, split_heads(value_block), preferred_element_type=FLOAT
    )
    grad_probs = lax.optimization_barrier(grad_probs.astype(BFLOAT)).astype(FLOAT)
    centre = jnp.sum(probs * grad_probs, axis=-1, keepdims=True)
    grad_scores = (probs * (grad_probs - centre)).astype(BFLOAT)
    grad_query = 0.125 * jnp.einsum(
        "shqk,skhd->sqhd", grad_scores, split_heads(key_block), preferred_element_type=FLOAT
    )
    grad_key = 0.125 * jnp.einsum(
        "shqk,sqhd->skhd", grad_scores, split_heads(query_block), preferred_element_type=FLOAT
    )
    grad_value = jnp.einsum(
        "shqk,sqhd->skhd", probs.astype(BFLOAT), grad_heads, preferred_element_type=FLOAT
    )
    shape = (query_block.shape[0], query_block.shape[1], -1)
    return tuple(
        (item.reshape(shape).astype(BFLOAT) for item in (grad_query, grad_key, grad_value))
    )


def layer_pass(seq_tokens, seq_cot, seg_rows, weights):
    (
        first_gain,
        first_bias,
        query_weight,
        key_weight,
        value_weight,
        out_weight,
        second_gain,
        second_bias,
        up_weight,
        up_bias,
        down_weight,
        down_bias,
    ) = weights
    seqs, length, width = seq_tokens.shape
    rows = seqs * length
    block = min(512, rows)
    blocks = rows // block
    within = block // length
    scale = 0.5
    inputs = seq_tokens.reshape(rows, width).astype(FLOAT)
    normed_one = norm_rows(inputs, first_gain, first_bias).astype(BFLOAT)
    query = product(normed_one, query_weight).astype(BFLOAT)
    key_rows = product(normed_one, key_weight).astype(BFLOAT)
    value_rows = product(normed_one, value_weight).astype(BFLOAT)
    labels = seg_rows.reshape(blocks, within, length)

    def split_rows(array):
        return array.reshape(blocks, within, length, -1)

    mixed = lax.map(
        block_forward, (split_rows(query), split_rows(key_rows), split_rows(value_rows), labels)
    )
    mixed = mixed.reshape(rows, -1)
    branch = product(mixed, out_weight)
    branch = lax.psum(branch, "gy")
    resid = inputs + branch
    normed_two = norm_rows(resid, second_gain, second_bias).astype(BFLOAT)
    pre_act = product(normed_two, up_weight) + up_bias
    hidden = jax.nn.gelu(pre_act).astype(BFLOAT)
    out_part = scale * (resid + down_bias) + product(hidden, down_weight)
    cot_rows = seq_cot.reshape(rows, width)
    cot_float = cot_rows.astype(FLOAT)
    down_bias_part = jnp.sum(cot_float, axis=0)
    down_part = inner(hidden, cot_rows)
    d_hidden = outer(cot_rows, down_weight)
    act_input = product(normed_two, up_weight) + up_bias
    _, gelu_pull = jax.vjp(jax.nn.gelu, act_input)
    d_pre = gelu_pull(d_hidden)[0].astype(BFLOAT)
    up_bias_part = jnp.sum(d_pre.astype(FLOAT), axis=0)
    up_part = inner(normed_two, d_pre)
    d_normed_two = outer(d_pre, up_weight)
    d_normed_two = lax.psum(d_normed_two, "gy")
    _, second_pull = jax.vjp(norm_rows, resid, second_gain, second_bias)
    d_resid_norm, second_gain_part, second_bias_part = second_pull(d_normed_two)
    d_resid = cot_float + d_resid_norm
    d_branch = d_resid.astype(BFLOAT)
    out_part_grad = inner(mixed, d_branch)
    d_mixed = outer(d_branch, out_weight).astype(BFLOAT)
    d_query, d_key, d_value = lax.map(
        block_backward,
        (
            split_rows(query),
            split_rows(key_rows),
            split_rows(value_rows),
            labels,
            split_rows(d_mixed),
        ),
    )
    d_query = d_query.reshape(rows, -1)
    d_key = d_key.reshape(rows, -1)
    d_value = d_value.reshape(rows, -1)
    query_part = inner(normed_one, d_query)
    key_part = inner(normed_one, d_key)
    value_part = inner(normed_one, d_value)
    d_normed_one = (
        outer(d_query, query_weight) + outer(d_key, key_weight) + outer(d_value, value_weight)
    )
    _, first_pull = jax.vjp(norm_rows, inputs, first_gain, first_bias)
    d_input_norm, first_gain_part, first_bias_part = first_pull(d_normed_one)
    d_tokens_part = scale * d_resid + d_input_norm
    parts = (
        first_gain_part,
        first_bias_part,
        query_part,
        key_part,
        value_part,
        out_part_grad,
        second_gain_part,
        second_bias_part,
        up_part,
        up_bias_part,
        down_part,
        down_bias_part,
    )
    return (
        out_part.reshape(seqs, length, width),
        d_tokens_part.reshape(seqs, length, width),
        parts,
    )


def per_device(
    latents,
    actions,
    segment_ids,
    cotangent,
    stem_weight,
    action_table,
    first_gain,
    first_bias,
    query_weight,
    key_weight,
    value_weight,
    out_weight,
    second_gain,
    second_bias,
    up_weight,
    up_bias,
    down_weight,
    down_bias,
):
    half_seqs, local_len, groups = latents.shape
    frames = half_seqs * local_len
    classes = stem_weight.shape[0] // groups
    latent_hot = (latents[..., None] == jnp.arange(classes, dtype=jnp.int32)).reshape(
        frames, groups * classes
    )
    latent_hot = latent_hot.astype(BFLOAT)
    action_hot = (
        actions.reshape(frames, 1) == jnp.arange(action_table.shape[0], dtype=jnp.int32)[None, :]
    )
    action_hot = action_hot.astype(BFLOAT)
    stem = product(latent_hot, stem_weight) + product(action_hot, action_table)
    tokens = stem.astype(BFLOAT).reshape(half_seqs, local_len, -1)
    token_all, cot_all = (
        lax.all_gather(tokens, "gy", axis=0, tiled=True),
        lax.all_gather(cotangent, "gy", axis=0, tiled=True),
    )
    seq_tokens, seq_cot = (
        lax.all_to_all(token_all, "gx", split_axis=0, concat_axis=1, tiled=True),
        lax.all_to_all(cot_all, "gx", split_axis=0, concat_axis=1, tiled=True),
    )
    seqs = seq_tokens.shape[0]
    first_seq = lax.axis_index("gx") * seqs
    weights = (
        first_gain,
        first_bias,
        query_weight,
        key_weight,
        value_weight,
        out_weight,
        second_gain,
        second_bias,
        up_weight,
        up_bias,
        down_weight,
        down_bias,
    )
    seg_rows = lax.dynamic_slice_in_dim(segment_ids, first_seq, seqs, 0)
    out_seq, grad_seq, parts = layer_pass(seq_tokens, seq_cot, seg_rows, weights)
    out_moved, grad_moved = (
        lax.all_to_all(out_seq, "gx", split_axis=1, concat_axis=0, tiled=True),
        lax.all_to_all(grad_seq, "gx", split_axis=1, concat_axis=0, tiled=True),
    )
    out_frames, grad_frames = (
        lax.psum_scatter(out_moved, "gy", scatter_dimension=0, tiled=True),
        lax.psum_scatter(grad_moved, "gy", scatter_dimension=0, tiled=True),
    )
    output = out_frames.astype(BFLOAT)
    token_grad = grad_frames.astype(BFLOAT)
    width = stem_weight.shape[1]
    grad_flat = token_grad.reshape(frames, width)
    stem_part = inner(latent_hot, grad_flat)
    action_part = inner(action_hot, grad_flat)
    (
        first_gain_part,
        first_bias_part,
        query_part,
        key_part,
        value_part,
        out_part_grad,
        second_gain_part,
        second_bias_part,
        up_part,
        up_bias_part,
        down_part,
        down_bias_part,
    ) = parts
    stem_grad, action_grad, first_gain_grad, first_bias_grad = lax.psum(
        (stem_part, action_part, first_gain_part, first_bias_part), ("gx", "gy")
    )
    (
        query_grad,
        key_grad,
        value_grad,
        out_grad,
        second_gain_grad,
        second_bias_grad,
        up_grad,
        up_bias_grad,
        down_grad,
        down_bias_grad,
    ) = lax.psum(
        (
            query_part,
            key_part,
            value_part,
            out_part_grad,
            second_gain_part,
            second_bias_part,
            up_part,
            up_bias_part,
            down_part,
            down_bias_part,
        ),
        "gx",
    )
    return (
        output,
        token_grad,
        stem_grad,
        action_grad,
        first_gain_grad,
        first_bias_grad,
        query_grad,
        key_grad,
        value_grad,
        out_grad,
        second_gain_grad,
        second_bias_grad,
        up_grad,
        up_bias_grad,
        down_grad,
        down_bias_grad,
    )


def solution(mesh):
    return jax.shard_map(
        per_device,
        mesh=mesh,
        in_specs=(
            P("gy", "gx", None),
            P("gy", "gx"),
            P(),
            P("gy", "gx", None),
            P(),
            P(),
            P(),
            P(),
            P(None, "gy"),
            P(None, "gy"),
            P(None, "gy"),
            P("gy", None),
            P(),
            P(),
            P(None, "gy"),
            P("gy"),
            P("gy", None),
            P(),
        ),
        out_specs=(
            P("gy", "gx", None),
            P("gy", "gx", None),
            P(),
            P(),
            P(),
            P(),
            P(None, "gy"),
            P(None, "gy"),
            P(None, "gy"),
            P("gy", None),
            P(),
            P(),
            P(None, "gy"),
            P("gy"),
            P("gy", None),
            P(),
        ),
        check_vma=False,
    )
```

profile of v0, /device:TPU:0, one launch (start us, length us, event | category | flops | bytes accessed | tf_op | source)
XLA Modules:
  0.0 1381.9 jit_solution(16798744642058293899)
XLA Ops:
  8.6 9.8 eq.86
  18.4 19.9 %eq.87 = s32[1536,1024]{1,0:T(8,128)} reshape(s32[384,4,32,32]{3,2,1,0:T(8,128)} %eq.86) | data formatting | bytes 12582912 | tf_op jit(solution)/shard_map/eq | solution.py:210
  46.1 47.8 %all-gather.3.cloned.1.call-done = bf16[768,4,512]{2,1,0:T(4,128)(2,1)} async-done(((bf16[384,4,512]{2,1,0:T(4,128)(2,1)}), bf16[768,4,512]{2,1,0:T(4,128)(2,1)}) %all-gather.3.cloned.1.call-update) | async-done | bytes 3145744 | tf_op jit(solution)/shard_map/all_gather | solution.py:221
  101.8 57.1 %all-to-all-done = bf16[768,4,512]{2,1,0:T(4,128)(2,1)} async-done(((bf16[768,4,512]{2,1,0:T(4,128)(2,1)}), bf16[768,4,512]{2,1,0:T(4,128)(2,1)}, u32[]{:S(2)}, u32[]{:S(2)}) %all-to-all-start) | async-done | bytes 3145760 | tf_op jit(solution)/shard_map/all_to_all | solution.py:225
  193.5 43.5 %while.24 = (s32[]{:T(128)}, bf16[6,8,64,256]{3,2,1,0:T(8,128)(2,1)}, bf16[6,8,64,256]{3,2,1,0:T(8,128)(2,1)}, s32[6,8,64]{2,1,0:T(8,128)S(1)}, bf16[6,8,64,256]...) while((s32[]{:T(128)}, bf16[6,8,64,256]{3,2,1,0:T(8,128)(2,1)}, ...), condition=%wide.region_5.6_spmd, body=%wide.region_2.5_spmd.sunk | while | flops 34674816 | bytes 9009781 | solution.py:115
  242.1 85.4 %all_to_all.60 = bf16[768,4,512]{2,1,0:T(4,128)(2,1)S(1)} all-to-all(bf16[768,4,512]{2,1,0:T(4,128)(2,1)} %all-gather.5.cloned.1.call-done), channel_id=1, replica_groups=mesh['gx'=16,'gy'=2] {'gx'}, dimensions={0} | all-to-all | bytes 6291456 | tf_op jit(solution)/shard_map/all_to_all | solution.py:226
  338.2 67.0 %all-reduce.12.cloned.1.call-done = f32[3072,512]{1,0:T(8,128)} async-done(((f32[3072,512]{1,0:T(8,128)}), f32[3072,512]{1,0:T(8,128)}) %all-reduce.12.cloned.1.call-update) | async-done | bytes 6291472 | tf_op jit(solution)/shard_map/psum | solution.py:120
  412.7 9.9 multiply_convert_fusion
  422.7 13.3 convert_reduce_fusion
  445.0 9.6 multiply_add_fusion
  467.1 130.6 %all-reduce.14.cloned.1.call-done = f32[3072,512]{1,0:T(8,128)} async-done(((f32[3072,512]{1,0:T(8,128)}), f32[3072,512]{1,0:T(8,128)}) %all-reduce.14.cloned.1.call-update) | async-done | bytes 6291472 | tf_op jit(solution)/shard_map/psum | solution.py:137
  618.5 89.6 %while.25 = (s32[]{:T(128)}, bf16[6,8,64,256]{3,2,1,0:T(8,128)(2,1)}, bf16[6,8,64,256]{3,2,1,0:T(8,128)(2,1)}, bf16[6,8,64,256]{3,2,1,0:T(8,128)(2,1)}, bf16[6,8...) while((s32[]{:T(128)}, ...), condition=%wide.region_17.18_spmd, body=%wide.region_13.17_spmd.sunk | while | flops 86839424 | bytes 17955988 | solution.py:144
  716.4 8.2 multiply_reduce_fusion.1
  744.0 9.9 iota_compare_fusion.2
  753.9 15.2 %eq.98 = pred[1536,1024]{1,0:T(32,128)(4,1)} reshape(pred[384,4,32,32]{3,2,1,0:T(32,128)(4,1)} %iota_compare_fusion.2) | data formatting | bytes 3145728 | tf_op jit(solution)/shard_map/eq | solution.py:210
  781.7 8.6 fusion.55
  790.3 7.8 fusion.39
  805.8 9.7 copy.109
  815.5 58.3 %all-to-all-done.3 = f32[48,64,512]{2,0,1:T(8,128)} async-done(((f32[48,64,512]{2,0,1:T(8,128)}), f32[48,64,512]{2,0,1:T(8,128)}, u32[]{:S(2)}, u32[]{:S(2)}) %all-to-all-start.3) | async-done | bytes 6291488 | tf_op jit(solution)/shard_map/all_to_all | solution.py:248
  873.8 9.6 copy.114
  883.4 290.4 %all-reduce.19 = (bf16[768,4,512]{2,1,0:T(4,128)(2,1)}, bf16[768,4,512]{2,1,0:T(4,128)(2,1)}) all-reduce(f32[768,4,512]{2,1,0:T(4,128)} %bitcast.176, f32[768,4,512]{2,1,0:T(4,128)} %bitcast.177), channel_id=2, replica_groups=mesh['gx'=16,'gy'=2] {'gy'}, use_global_device_ids=true, to_apply=%region_9.10.clone | all-reduce | flops 3145728 | bytes 18874368
  1187.1 102.3 %all-reduce.3 = (f32[512]{0:T(512)}, f32[512]{0:T(512)}, f32[1024]{0:T(1024)}, f32[512]{0:T(512)}) all-reduce(f32[512]{0:T(512)S(1)} %get-tuple-element.146, f32[512]{0:T(512)S(1)} %get-tuple-element.150, f32[1024]{0:T(1024)S(1)} %copy-done.49, f32[512]{0:T(512)S(1)} %convert_reduce_fusion.1), channel_id=1, replica_groups=mesh['gx'=16,'gy'=2] {'gx'}, use_global_device_ids=true, to_apply=%region_32.33 | all-reduce | flops 2560 | bytes 20480 | tf_op jit(solution)/shard_map/psum | solution.py:288
  1289.9 37.9 %all-reduce.2 = (f32[18,512]{1,0:T(8,128)}, f32[512]{0:T(512)}, f32[512]{0:T(512)}) all-reduce(f32[18,512]{1,0:T(8,128)S(1)} %fusion.33, f32[512]{0:T(512)S(1)} %get-tuple-element.148, f32[512]{0:T(512)S(1)} %get-tuple-element.151), channel_id=1, replica_groups=mesh['gx'=16,'gy'=2] {'gx','gy'}, use_global_device_ids=true, to_apply=%region_22.23 | all-reduce | flops 10240 | bytes 81920 | tf_op jit(solution)/shard_map/psum | solution.py:274
  1331.0 32.4 %all-reduce.16.cloned.1.call-done = f32[1024,512]{1,0:T(8,128)} async-done(((f32[1024,512]{1,0:T(8,128)}), f32[1024,512]{1,0:T(8,128)}) %all-reduce.16.cloned.1.call-update) | async-done | bytes 2097168 | tf_op jit(solution)/shard_map/psum | solution.py:274
  (472 shorter events, 323.8 us)
Async XLA Ops:
  7.2 405.5 %copy-start = (bf16[512,1024]{1,0:T(8,128)(2,1)S(1)}, bf16[512,1024]{1,0:T(8,128)(2,1)}, u32[]{:S(2)}) copy-start(bf16[512,1024]{1,0:T(8,128)(2,1)} %param.36) | copy-start | bytes 3145732
  7.2 86.7 %all-gather.3.cloned.1.call-start = ((), (), s32[]{:S(2)}) async-start(), calls=%async_computation.4 | async-start | bytes 4718592 | tf_op jit(solution)/shard_map/all_gather | solution.py:221
  18.4 20.0 %copy-start.48 = (s32[384,4]{0,1:T(4,128)S(1)}, s32[384,4]{0,1:T(4,128)}, u32[]{:S(2)}) copy-start(s32[384,4]{0,1:T(4,128)} %param.23) | copy-start | bytes 18436
  93.9 65.1 %all-to-all-start = ((bf16[768,4,512]{2,1,0:T(4,128)(2,1)}), bf16[768,4,512]{2,1,0:T(4,128)(2,1)}, u32[]{:S(2)}, u32[]{:S(2)}) async-start(bf16[768,4,512]{2,1,0:T(4,128)(2,1)} %all-gather.3.cloned.1.call-done), calls=%async_computation | async-start | bytes 6291456 | tf_op jit(solution)/shard_map/all_to_all | solution.py:225
  99.5 142.6 %all-gather.5.cloned.1.call-start = ((), (), s32[]{:S(2)}) async-start(), calls=%async_computation.6 | async-start | bytes 4718592 | tf_op jit(solution)/shard_map/all_gather | solution.py:222
  100.3 304.9 %all-reduce.12.cloned.1.call-start = ((), (), s32[]{:S(2)}) async-start(), calls=%async_computation.5 | async-start | bytes 12582912 | tf_op jit(solution)/shard_map/psum | solution.py:120
  166.9 15.1 %copy-start.34 = (f32[3072]{0:T(1024)}, f32[3072]{0:T(1024)S(1)}, u32[]{:S(2)}) copy-start(f32[3072]{0:T(1024)S(1)} %div.59) | copy-start | bytes 36868
  193.5 43.5 %copy-start.30 = (bf16[256,512]{1,0:T(8,128)(2,1)S(1)}, bf16[256,512]{1,0:T(8,128)(2,1)}, u32[]{:S(2)}) copy-start(bf16[256,512]{1,0:T(8,128)(2,1)} %param.33) | copy-start | bytes 786436
  242.0 355.7 %all-reduce.14.cloned.1.call-start = ((), (), s32[]{:S(2)}) async-start(), calls=%async_computation.7 | async-start | bytes 12582912 | tf_op jit(solution)/shard_map/psum | solution.py:137
  410.5 12.2 copy-start.3
  461.0 277.1 %all-to-all-start.1 = ((f32[48,64,512]{2,0,1:T(8,128)}), f32[48,64,512]{2,0,1:T(8,128)}, u32[]{:S(2)}, u32[]{:S(2)}) async-start(f32[48,64,512]{2,0,1:T(8,128)} %copy.108), calls=%async_computation.1 | async-start | bytes 12582912 | tf_op jit(solution)/shard_map/all_to_all | solution.py:247
  710.8 19.4 %slice-start.4 = ((s8[6291456]{0:T(1024)(128)(4,1)}), s8[4194304]{0:T(1024)(128)(4,1)S(1)}, s32[]{:S(2)}) async-start(s8[6291456]{0:T(1024)(128)(4,1)} %bitcast.170), calls=%async_computation.14 | async-start | bytes 8388608
  716.4 13.8 slice-start.5
  738.1 135.6 %all-to-all-start.3 = ((f32[48,64,512]{2,0,1:T(8,128)}), f32[48,64,512]{2,0,1:T(8,128)}, u32[]{:S(2)}, u32[]{:S(2)}) async-start(f32[48,64,512]{2,0,1:T(8,128)} %copy.113), calls=%async_computation.3 | async-start | bytes 12582912 | tf_op jit(solution)/shard_map/all_to_all | solution.py:248
  743.9 587.0 %all-reduce.18.cloned.1.call-start = ((), (), s32[]{:S(2)}) async-start(), calls=%async_computation.9 | async-start | bytes 12582912 | tf_op jit(solution)/shard_map/psum | solution.py:288
  744.0 25.1 %copy-start.55 = (u32[32]{0:T(128)S(1)}, u32[32]{0:T(128)}, u32[]{:S(2)}) copy-start(u32[32]{0:T(128)} %constant.93) | copy-start | bytes 388
  744.0 26.4 %copy-start.20 = (f32[48,16,4]{2,1,0:T(8,128)S(1)}, f32[48,16,4]{2,1,0:T(8,128)}, u32[]{:S(2)}) copy-start(f32[48,16,4]{2,1,0:T(8,128)} %copy-done.19) | copy-start | bytes 36868
  744.0 26.4 %copy-start.25 = (f32[48,16,4]{2,1,0:T(8,128)S(1)}, f32[48,16,4]{2,1,0:T(8,128)}, u32[]{:S(2)}) copy-start(f32[48,16,4]{2,1,0:T(8,128)} %get-tuple-element.209) | copy-start | bytes 36868
  744.0 26.4 %copy-start.46 = (f32[512]{0:T(512)S(1)}, f32[512]{0:T(512)}, u32[]{:S(2)}) copy-start(f32[512]{0:T(512)} %param.29) | copy-start | bytes 6148
  776.0 14.3 %slice-start.2 = ((s8[6291456]{0:T(1024)(128)(4,1)}), s8[2097152]{0:T(1024)(128)(4,1)S(1)}, s32[]{:S(2)}) async-start(s8[6291456]{0:T(1024)(128)(4,1)} %bitcast.168), calls=%async_computation.12 | async-start | bytes 4194304
  805.5 557.9 %all-reduce.16.cloned.1.call-start = ((), (), s32[]{:S(2)}) async-start(), calls=%async_computation.8 | async-start | bytes 4194304 | tf_op jit(solution)/shard_map/psum | solution.py:274
  1179.2 110.2 %copy-start.41 = (s32[1536]{0:T(1024)S(1)}, s32[1536]{0:T(1024)}, u32[]{:S(2)}) copy-start(s32[1536]{0:T(1024)} %copy-done.40) | copy-start | bytes 18436
  1331.0 41.0 %copy-start.24 = (f32[512,1024]{1,0:T(8,128)S(1)}, f32[512,1024]{1,0:T(8,128)}, u32[]{:S(2)}) copy-start(f32[512,1024]{1,0:T(8,128)} %get-tuple-element.383) | copy-start | bytes 6291460
  1363.4 11.2 copy-start.1
  (59 other events, 275.7 us)
Sparse Core Ops, SparseCore 0:
  46.2 47.6 all-gather.2
  101.9 45.2 all-gather.4
  242.1 162.9 all-reduce.11
  444.5 153.1 all-reduce.13
  805.6 207.0 all-reduce.17
  1183.9 179.4 all-reduce.15
where the time goes:
time: 1390 us; the launch traced here: 1380 us
  blocking collectives  516 us (37%)
  waiting for transfers between devices  394 us (28%)
  local copies, waits for them, and re-layouts  220 us (16%)
  matrix products  136 us (10%)
  other arithmetic  80.5 us (6%)
  starting transfers between devices  18.5 us (1%)
  between operations  16 us (1%)
    unnamed x1, blocking collectives  290 us
    psum x1, waiting for transfers between devices, layer_pass(): d_normed_two = lax.psum(d_normed_two, 'gy')  131 us
    psum x1, blocking collectives, per_device(): lax.psum((query_part, key_part, value_part, out_part_grad, second_gain_pa...  102 us
    all_to_all x1, blocking collectives, per_device(): lax.all_to_all(cot_all, 'gx', split_axis=0, concat_axis=1, tiled=True)  85.4 us
    psum x1, waiting for transfers between devices, layer_pass(): branch = lax.psum(branch, 'gy')  67 us
    all_to_all x1, waiting for transfers between devices, per_device(): lax.all_to_all(grad_seq, 'gx', split_axis=1, concat_axis=0, tiled=True)  58.3 us
    all_to_all x1, waiting for transfers between devices, per_device(): lax.all_to_all(token_all, 'gx', split_axis=0, concat_axis=1, tiled=True)  57.1 us
    all_gather x1, waiting for transfers between devices, per_device(): lax.all_gather(tokens, 'gy', axis=0, tiled=True)  47.8 us
  transfers between devices with their start and end apart: 9, of which 6 were waited for; matrix products, arithmetic and copies ran while one was open for 24% of the time, Pallas kernels for 0%

commit v1 on v0

--- a/solution.py
+++ b/solution.py
@@ -272,7 +272,7 @@
         down_bias_part,
     ) = parts
     stem_grad, action_grad, first_gain_grad, first_bias_grad = lax.psum(
-        (stem_part, action_part, first_gain_part, first_bias_part), ("gx", "gy")
+        lax.psum((stem_part, action_part, first_gain_part, first_bias_part), "gy"), "gx"
     )
     (
         query_grad,

time: 1390 us -> 1400 us (level)
  blocking collectives: 516 us -> 443 us
  waiting for transfers between devices: 394 us -> 436 us
  starting transfers between devices: 18.5 us -> 40.2 us
    psum x2 -> x1, blocking collectives: 140 us -> 61.1 us  [per_device(): lax.psum(lax.psum((stem_part, action_part, first_gain_part, first_bias_pa...]
    psum x1, waiting for transfers between devices: 131 us -> 153 us  [layer_pass(): d_normed_two = lax.psum(d_normed_two, 'gy')]
    all_to_all x1, starting transfers between devices: 6.08 us -> 28.1 us  [per_device(): lax.all_to_all(out_seq, 'gx', split_axis=1, concat_axis=0, tiled=True)]
    all_to_all x1, waiting for transfers between devices: 58.3 us -> 72.7 us  [per_device(): lax.all_to_all(grad_seq, 'gx', split_axis=1, concat_axis=0, tiled=True)]
    unnamed x1 -> x2, blocking collectives: 290 us -> 297 us
  transfers between devices with their start and end apart: 9 -> 9, of which waited for: 6 -> 6; matrix products, arithmetic and copies ran while one was open for 24% -> 15% of each run, Pallas kernels for 0% -> 0%
where the time goes in v1:
time: 1400 us; the launch traced here: 1390 us
  blocking collectives  443 us (32%)
  waiting for transfers between devices  436 us (31%)
  local copies, waits for them, and re-layouts  228 us (16%)
  matrix products  143 us (10%)
  other arithmetic  81.1 us (6%)
  starting transfers between devices  40.2 us (3%)
  between operations  15.7 us (1%)
    unnamed x2, blocking collectives  297 us
    psum x1, waiting for transfers between devices, layer_pass(): d_normed_two = lax.psum(d_normed_two, 'gy')  153 us
    all_to_all x1, blocking collectives, per_device(): lax.all_to_all(cot_all, 'gx', split_axis=0, concat_axis=1, tiled=True)  85.5 us
    all_to_all x1, waiting for transfers between devices, per_device(): lax.all_to_all(grad_seq, 'gx', split_axis=1, concat_axis=0, tiled=True)  72.7 us
    psum x1, waiting for transfers between devices, layer_pass(): branch = lax.psum(branch, 'gy')  66.8 us
    psum x1, blocking collectives, per_device(): lax.psum(lax.psum((stem_part, action_part, first_gain_part, first_bias_pa...  61.1 us
    all_to_all x1, waiting for transfers between devices, per_device(): lax.all_to_all(token_all, 'gx', split_axis=0, concat_axis=1, tiled=True)  57.5 us
    all_gather x1, waiting for transfers between devices, per_device(): lax.all_gather(tokens, 'gy', axis=0, tiled=True)  47.8 us
  transfers between devices with their start and end apart: 9, of which 6 were waited for; matrix products, arithmetic and copies ran while one was open for 15% of the time, Pallas kernels for 0%

profile of v1, /device:TPU:0, one launch (start us, length us, event | category | flops | bytes accessed | tf_op | source)
XLA Modules:
  0.0 1388.6 jit_solution(12989979130121625153)
XLA Ops:
  9.6 9.8 eq.86
  19.4 19.9 %eq.87 = s32[1536,1024]{1,0:T(8,128)} reshape(s32[384,4,32,32]{3,2,1,0:T(8,128)} %eq.86) | data formatting | bytes 12582912 | tf_op jit(solution)/shard_map/eq | solution.py:210
  46.7 47.8 %all-gather.3.cloned.1.call-done = bf16[768,4,512]{2,1,0:T(4,128)(2,1)} async-done(((bf16[384,4,512]{2,1,0:T(4,128)(2,1)}), bf16[768,4,512]{2,1,0:T(4,128)(2,1)}) %all-gather.3.cloned.1.call-update) | async-done | bytes 3145744 | tf_op jit(solution)/shard_map/all_gather | solution.py:221
  102.2 57.5 %all-to-all-done = bf16[768,4,512]{2,1,0:T(4,128)(2,1)} async-done(((bf16[768,4,512]{2,1,0:T(4,128)(2,1)}), bf16[768,4,512]{2,1,0:T(4,128)(2,1)}, u32[]{:S(2)}, u32[]{:S(2)}) %all-to-all-start) | async-done | bytes 3145760 | tf_op jit(solution)/shard_map/all_to_all | solution.py:225
  194.0 45.5 %while.24 = (s32[]{:T(128)}, bf16[6,8,64,256]{3,2,1,0:T(8,128)(2,1)}, bf16[6,8,64,256]{3,2,1,0:T(8,128)(2,1)}, s32[6,8,64]{2,1,0:T(8,128)S(1)}, bf16[6,8,64,256]...) while((s32[]{:T(128)}, bf16[6,8,64,256]{3,2,1,0:T(8,128)(2,1)}, ...), condition=%wide.region_5.6_spmd, body=%wide.region_2.5_spmd.sunk | while | flops 34674816 | bytes 9009281 | solution.py:115
  244.6 85.5 %all_to_all.60 = bf16[768,4,512]{2,1,0:T(4,128)(2,1)S(1)} all-to-all(bf16[768,4,512]{2,1,0:T(4,128)(2,1)} %all-gather.5.cloned.1.call-done), channel_id=1, replica_groups=mesh['gx'=16,'gy'=2] {'gx'}, dimensions={0} | all-to-all | bytes 6291456 | tf_op jit(solution)/shard_map/all_to_all | solution.py:226
  340.9 66.8 %all-reduce.12.cloned.1.call-done = f32[3072,512]{1,0:T(8,128)} async-done(((f32[3072,512]{1,0:T(8,128)}), f32[3072,512]{1,0:T(8,128)}) %all-reduce.12.cloned.1.call-update) | async-done | bytes 6291472 | tf_op jit(solution)/shard_map/psum | solution.py:120
  415.3 9.9 multiply_convert_fusion
  425.1 13.3 convert_reduce_fusion
  446.9 153.4 %all-reduce.14.cloned.1.call-done = f32[3072,512]{1,0:T(8,128)} async-done(((f32[3072,512]{1,0:T(8,128)}), f32[3072,512]{1,0:T(8,128)}) %all-reduce.14.cloned.1.call-update) | async-done | bytes 6291472 | tf_op jit(solution)/shard_map/psum | solution.py:137
  621.0 100.7 %while.25 = (s32[]{:T(128)}, bf16[6,8,64,256]{3,2,1,0:T(8,128)(2,1)}, bf16[6,8,64,256]{3,2,1,0:T(8,128)(2,1)}, bf16[6,8,64,256]{3,2,1,0:T(8,128)(2,1)}, bf16[6,8...) while((s32[]{:T(128)}, ...), condition=%wide.region_17.18_spmd, body=%wide.region_13.17_spmd.sunk | while | flops 86839424 | bytes 17954980 | solution.py:144
  757.6 9.9 iota_compare_fusion.2
  767.5 15.2 %eq.98 = pred[1536,1024]{1,0:T(32,128)(4,1)} reshape(pred[384,4,32,32]{3,2,1,0:T(32,128)(4,1)} %iota_compare_fusion.2) | data formatting | bytes 3145728 | tf_op jit(solution)/shard_map/eq | solution.py:210
  783.9 8.8 multiply_add_fusion
  799.1 72.7 %all-to-all-done.3 = f32[48,64,512]{2,0,1:T(8,128)} async-done(((f32[48,64,512]{2,0,1:T(8,128)}), f32[48,64,512]{2,0,1:T(8,128)}, u32[]{:S(2)}, u32[]{:S(2)}) %all-to-all-start.3) | async-done | bytes 6291488 | tf_op jit(solution)/shard_map/all_to_all | solution.py:248
  871.7 28.1 %all-to-all-start.1 = ((f32[48,64,512]{2,0,1:T(8,128)}), f32[48,64,512]{2,0,1:T(8,128)}, u32[]{:S(2)}, u32[]{:S(2)}) async-start(f32[48,64,512]{2,0,1:T(8,128)} %copy.108), calls=%async_computation.1 | async-start | bytes 12582912 | tf_op jit(solution)/shard_map/all_to_all | solution.py:247
  914.7 9.5 fusion.39
  924.2 9.6 copy.114
  933.8 148.2 %all-reduce.19 = bf16[768,4,512]{2,1,0:T(4,128)(2,1)} all-reduce(f32[768,4,512]{2,1,0:T(4,128)} %bitcast.175), channel_id=3, replica_groups=mesh['gx'=16,'gy'=2] {'gy'}, use_global_device_ids=true, to_apply=%region_20.21.clone | all-reduce | flops 1572864 | bytes 9437184
  1093.9 8.6 fusion.55
  1109.8 9.7 copy.109
  1120.2 37.2 %all-reduce.16.cloned.1.call-done = f32[1024,512]{1,0:T(8,128)} async-done(((f32[1024,512]{1,0:T(8,128)}), f32[1024,512]{1,0:T(8,128)}) %all-reduce.16.cloned.1.call-update) | async-done | bytes 2097168 | tf_op jit(solution)/shard_map/psum | solution.py:275
  1157.4 148.7 %all-reduce.20 = (bf16[768,4,512]{2,1,0:T(4,128)(2,1)}, f32[18,512]{1,0:T(8,128)S(1)}, f32[512]{0:T(512)S(1)}, f32[512]{0:T(512)S(1)}) all-reduce(f32[768,4,512]{2,1,0:T(4,128)} %bitcast.174, f32[18,512]{1,0:T(8,128)S(1)} %fusion.33, f32[512]{0:T(512)S(1)} %get-tuple-element.148, ...), channel_id=2, replica_groups=mesh['gx'=16,'gy'=2] {'gy'}, use_global_device_ids=true, to_apply=%region_9.10.clone | all-reduce | flops 1583104 | bytes 9519104
  1306.1 61.1 %all-reduce.2 = (f32[18,512]{1,0:T(8,128)}, f32[512]{0:T(512)}, f32[512]{0:T(512)}, f32[512]{0:T(512)}, f32[512]{0:T(512)}, /*index=5*/f32[1024]{0:T(1024)}, f32[512]{0:T(512)}) all-reduce(f32[18,512]{1,0:T(8,128)S(1)} %get-tuple-element.197, f32[512]{0:T(512)S(1)} %get-tuple-element.198, ...), channel_id=1, replica_groups=mesh['gx'=16,'gy'=2] {'gx'}, use_global_device_ids=true, to_apply=%region_24.25 | all-reduce | flops 12800 | bytes 102400 | tf_op jit(solution)/shard_map/psum | solution.py:274
  (467 shorter events, 340.7 us)
Async XLA Ops:
  7.2 408.0 %copy-start = (bf16[512,1024]{1,0:T(8,128)(2,1)S(1)}, bf16[512,1024]{1,0:T(8,128)(2,1)}, u32[]{:S(2)}) copy-start(bf16[512,1024]{1,0:T(8,128)(2,1)} %param.36) | copy-start | bytes 3145732
  7.2 87.3 %all-gather.3.cloned.1.call-start = ((), (), s32[]{:S(2)}) async-start(), calls=%async_computation.4 | async-start | bytes 4718592 | tf_op jit(solution)/shard_map/all_gather | solution.py:221
  8.4 35.8 %copy-start.41 = (s32[1536]{0:T(1024)}, s32[1536]{0:T(1024)S(1)}, u32[]{:S(2)}) copy-start(s32[1536]{0:T(1024)S(1)} %eq.92) | copy-start | bytes 18436
  94.5 65.1 %all-to-all-start = ((bf16[768,4,512]{2,1,0:T(4,128)(2,1)}), bf16[768,4,512]{2,1,0:T(4,128)(2,1)}, u32[]{:S(2)}, u32[]{:S(2)}) async-start(bf16[768,4,512]{2,1,0:T(4,128)(2,1)} %all-gather.3.cloned.1.call-done), calls=%async_computation | async-start | bytes 6291456 | tf_op jit(solution)/shard_map/all_to_all | solution.py:225
  100.2 144.4 %all-gather.5.cloned.1.call-start = ((), (), s32[]{:S(2)}) async-start(), calls=%async_computation.6 | async-start | bytes 4718592 | tf_op jit(solution)/shard_map/all_gather | solution.py:222
  100.9 306.8 %all-reduce.12.cloned.1.call-start = ((), (), s32[]{:S(2)}) async-start(), calls=%async_computation.5 | async-start | bytes 12582912 | tf_op jit(solution)/shard_map/psum | solution.py:120
  163.1 19.4 %copy-start.35 = (f32[3072]{0:T(1024)}, f32[3072]{0:T(1024)S(1)}, u32[]{:S(2)}) copy-start(f32[3072]{0:T(1024)S(1)} %div.59) | copy-start | bytes 36868
  194.0 45.5 %copy-start.30 = (bf16[256,512]{1,0:T(8,128)(2,1)S(1)}, bf16[256,512]{1,0:T(8,128)(2,1)}, u32[]{:S(2)}) copy-start(bf16[256,512]{1,0:T(8,128)(2,1)} %param.33) | copy-start | bytes 786436
  244.5 355.7 %all-reduce.14.cloned.1.call-start = ((), (), s32[]{:S(2)}) async-start(), calls=%async_computation.7 | async-start | bytes 12582912 | tf_op jit(solution)/shard_map/psum | solution.py:137
  413.0 12.1 copy-start.3
  621.0 100.7 %copy-start.32 = (bf16[512,256]{1,0:T(8,128)(2,1)S(1)}, bf16[512,256]{1,0:T(8,128)(2,1)}, u32[]{:S(2)}) copy-start(bf16[512,256]{1,0:T(8,128)(2,1)} %param.31) | copy-start | bytes 786436
  724.3 19.3 %slice-start.2 = ((s8[6291456]{0:T(1024)(128)(4,1)}), s8[4194304]{0:T(1024)(128)(4,1)S(1)}, s32[]{:S(2)}) async-start(s8[6291456]{0:T(1024)(128)(4,1)} %bitcast.168), calls=%async_computation.12 | async-start | bytes 8388608
  730.0 13.7 slice-start.3
  751.7 120.0 %all-to-all-start.3 = ((f32[48,64,512]{2,0,1:T(8,128)}), f32[48,64,512]{2,0,1:T(8,128)}, u32[]{:S(2)}, u32[]{:S(2)}) async-start(f32[48,64,512]{2,0,1:T(8,128)} %copy.113), calls=%async_computation.3 | async-start | bytes 12582912 | tf_op jit(solution)/shard_map/all_to_all | solution.py:248
  757.5 25.1 %copy-start.55 = (u32[32]{0:T(128)S(1)}, u32[32]{0:T(128)}, u32[]{:S(2)}) copy-start(u32[32]{0:T(128)} %constant.93) | copy-start | bytes 388
  757.5 26.4 %copy-start.52 = (f32[512]{0:T(512)S(1)}, f32[512]{0:T(512)}, u32[]{:S(2)}) copy-start(f32[512]{0:T(512)} %param.39) | copy-start | bytes 6148
  799.0 100.8 %copy-start.20 = (f32[48,16,4]{2,1,0:T(8,128)S(1)}, f32[48,16,4]{2,1,0:T(8,128)}, u32[]{:S(2)}) copy-start(f32[48,16,4]{2,1,0:T(8,128)} %copy-done.19) | copy-start | bytes 36868
  799.0 100.8 %copy-start.25 = (f32[48,16,4]{2,1,0:T(8,128)S(1)}, f32[48,16,4]{2,1,0:T(8,128)}, u32[]{:S(2)}) copy-start(f32[48,16,4]{2,1,0:T(8,128)} %get-tuple-element.212) | copy-start | bytes 36868
  799.0 100.9 %copy-start.47 = (f32[512]{0:T(512)S(1)}, f32[512]{0:T(512)}, u32[]{:S(2)}) copy-start(f32[512]{0:T(512)} %param.29) | copy-start | bytes 6148
  871.7 238.1 %all-to-all-start.1 = ((f32[48,64,512]{2,0,1:T(8,128)}), f32[48,64,512]{2,0,1:T(8,128)}, u32[]{:S(2)}, u32[]{:S(2)}) async-start(f32[48,64,512]{2,0,1:T(8,128)} %copy.108), calls=%async_computation.1 | async-start | bytes 12582912 | tf_op jit(solution)/shard_map/all_to_all | solution.py:247
  899.8 257.6 %all-reduce.16.cloned.1.call-start = ((), (), s32[]{:S(2)}) async-start(), calls=%async_computation.8 | async-start | bytes 4194304 | tf_op jit(solution)/shard_map/psum | solution.py:275
  1093.7 276.7 %all-reduce.18.cloned.1.call-start = ((), (), s32[]{:S(2)}) async-start(), calls=%async_computation.9 | async-start | bytes 16777216 | tf_op jit(solution)/shard_map/psum | solution.py:274
  1157.4 148.7 %copy-start.49 = (f32[1024]{0:T(1024)S(1)}, f32[1024]{0:T(1024)}, u32[]{:S(2)}) copy-start(f32[1024]{0:T(1024)} %get-tuple-element.217) | copy-start | bytes 12292
  1370.4 11.2 copy-start.1
  (57 other events, 273.9 us)
Sparse Core Ops, SparseCore 0:
  46.8 47.6 all-gather.2
  102.6 45.2 all-gather.4
  244.7 163.0 all-reduce.11
  447.0 153.1 all-reduce.13
  1093.8 63.5 all-reduce.15
  1163.8 172.7 all-reduce.17
